TPU v7x, 32 devices: a whole 2x2x4 slice. The times are simulated.
32 devices in a mesh: dp: 8 (over z, x), seq: 4 (over y, core).
Axes of the slice: x: 2, y: 2, z: 4, core: 2. Of those that a mesh axis runs over, the one named last changes fastest.
Arguments:
- hidden_in: bfloat16 [4096, 1024], P(('dp', 'seq')), may hold values from -6 to 6
- cotangent: bfloat16 [4096, 1024], P(('dp', 'seq')), may hold values from -6 to 6
- segments: int32 [8, 512], P('dp'), may hold values from 0 to 2, never falling along the last dimension, each value on 1 to 256 neighbouring positions
- shared_params: float32 [9216], P(('dp', 'seq')), as said below
- split_params: float32 [4, 3146752], P('seq', 'dp'), as said below
- shared_m1: float32 [9216], P(('dp', 'seq')), may hold values from -56 to 56
- split_m1: float32 [4, 3146752], P('seq', 'dp'), may hold values from -56 to 56
- shared_m2: float32 [9216], P(('dp', 'seq')), may hold values from 204.8 to 819.2
- split_m2: float32 [4, 3146752], P('seq', 'dp'), may hold values from 204.8 to 819.2
Outputs:
- output: bfloat16 [4096, 1024], P(('dp', 'seq'))
- input_grad: float32 [4096, 1024], P(('dp', 'seq'))
- shared_grads: float32 [9216], P(('dp', 'seq'))
- split_grads: float32 [4, 3146752], P('seq', 'dp')
- shared_new: float32 [9216], P(('dp', 'seq'))
- split_new: float32 [4, 3146752], P('seq', 'dp')
- shared_m1_new: float32 [9216], P(('dp', 'seq'))
- split_m1_new: float32 [4, 3146752], P('seq', 'dp')
- shared_m2_new: float32 [9216], P(('dp', 'seq'))
- split_m2_new: float32 [4, 3146752], P('seq', 'dp')
Inputs may be any that keep to these rules, and one draw needn't show every extreme that they name: `shared_params`: the 9216 entries are the shared parameters packed as the first step reads them. `split_params`: row s holds the share s of the qkv, dense, fc and proj parameters as the second step reads them.
All inputs are finite; a program needn't handle non-finite values.
Results may differ from a plain program's by a relative error of at most 0.007.
The roundings to bfloat16 on the way count: a program that leaves them out, or rounds other values in their place, can miss the bound.
Values may be sent and summed in bfloat16 or wider, within the bound.
A program may use at most 192 MiB of HBM per device.

v0:
```python
import math

import jax
import jax.numpy as jnp
from jax import lax
from jax.experimental import pallas as pl
from jax.experimental.pallas import tpu as pltpu
from jax.sharding import PartitionSpec as P

MODEL_WIDTH = 1024
HEADS = 16
HEAD_DIM = 64
FF = 4096
ROT = 16
STEP = 3


norm_eps = 1e-05
beta_first = 0.9
beta_second = 0.95
adam_eps = 1e-08
learn_rate = 0.1
weight_decay = 0.01
rotary_base = 10000.0
masked_score = -1e30


def unpack_shared(flat_vec):
    extents = [
        (3 * MODEL_WIDTH,),
        (MODEL_WIDTH,),
        (MODEL_WIDTH,),
        (MODEL_WIDTH,),
        (MODEL_WIDTH,),
        (MODEL_WIDTH,),
        (MODEL_WIDTH,),
    ]
    pieces = []
    offset = 0
    for extent in extents:
        number = math.prod(extent)
        pieces.append(flat_vec[offset : offset + number])
        offset = offset + number
    return pieces


def unpack_split(matrix, seq_count):
    rows = matrix.shape[0]
    qkv_part = 3 * MODEL_WIDTH // seq_count
    dense_output_slice = MODEL_WIDTH // seq_count
    hidden_units_slice = FF // seq_count
    zero_end = MODEL_WIDTH * qkv_part
    first_end = zero_end + dense_output_slice * MODEL_WIDTH
    second_end = first_end + MODEL_WIDTH * hidden_units_slice
    third_end = second_end + hidden_units_slice
    w_qkv = (
        matrix[:, :zero_end]
        .reshape(rows, MODEL_WIDTH, qkv_part)
        .transpose(1, 0, 2)
        .reshape(MODEL_WIDTH, rows * qkv_part)
    )
    dense_weight = matrix[:, zero_end:first_end].reshape(rows * dense_output_slice, MODEL_WIDTH)
    expand_weight = (
        matrix[:, first_end:second_end]
        .reshape(rows, MODEL_WIDTH, hidden_units_slice)
        .transpose(1, 0, 2)
        .reshape(MODEL_WIDTH, rows * hidden_units_slice)
    )
    b_fc = matrix[:, second_end:third_end].reshape(rows * hidden_units_slice)
    contract_weight = matrix[:, third_end:].reshape(rows * hidden_units_slice, MODEL_WIDTH)
    return (w_qkv, dense_weight, expand_weight, b_fc, contract_weight)


def pack_split(w_qkv, dense_weight, expand_weight, b_fc, contract_weight, seq_count):
    qkv_part = 3 * MODEL_WIDTH // seq_count
    dense_output_slice = MODEL_WIDTH // seq_count
    hidden_units_slice = FF // seq_count
    rows = dense_weight.shape[0] // dense_output_slice
    return jnp.concatenate(
        [
            w_qkv.reshape(MODEL_WIDTH, rows, qkv_part)
            .transpose(1, 0, 2)
            .reshape(rows, MODEL_WIDTH * qkv_part),
            dense_weight.reshape(rows, dense_output_slice * MODEL_WIDTH),
            expand_weight.reshape(MODEL_WIDTH, rows, hidden_units_slice)
            .transpose(1, 0, 2)
            .reshape(rows, MODEL_WIDTH * hidden_units_slice),
            b_fc.reshape(rows, hidden_units_slice),
            contract_weight.reshape(rows, hidden_units_slice * MODEL_WIDTH),
        ],
        1,
    )


def adamw(param_vals, first_m, second_m, grad_vals):
    first_new = beta_first * first_m + (1.0 - beta_first) * grad_vals
    second_new = beta_second * second_m + (1.0 - beta_second) * grad_vals * grad_vals
    first_hat = first_new / (1.0 - beta_first**STEP)
    second_hat = second_new / (1.0 - beta_second**STEP)
    param_new = param_vals - learn_rate * (
        first_hat / (jnp.sqrt(second_hat) + adam_eps) + weight_decay * param_vals
    )
    return (param_new, first_new, second_new)


def layer_norm(resid, gain_vec, shift_vec):
    average = jnp.mean(resid, -1, keepdims=True)
    centered = resid - average
    variance = jnp.mean(centered * centered, -1, keepdims=True)
    recip_root = lax.rsqrt(variance + norm_eps)
    normed = centered * recip_root
    return (normed * gain_vec + shift_vec, normed, recip_root)


def norm_back(grad_norm, gain_vec, normed, recip_root):
    scaled = grad_norm * gain_vec
    return recip_root * (
        scaled
        - jnp.mean(scaled, -1, keepdims=True)
        - normed * jnp.mean(scaled * normed, -1, keepdims=True)
    )


def gelu_slope(inputs):
    normal_cdf = 0.5 * (1.0 + jax.scipy.special.erf(inputs * 0.7071067811865476))
    return normal_cdf + inputs * jnp.exp(-0.5 * inputs * inputs) * 0.3989422804014327


def rotary_tables(segment_row):
    indices = jnp.arange(segment_row.shape[0], dtype=jnp.int32)
    change = jnp.concatenate([jnp.ones((1,), dtype=jnp.bool_), segment_row[1:] != segment_row[:-1]])
    starts = lax.cummax(jnp.where(change, indices, jnp.zeros_like(indices)), axis=0)
    positions = (indices - starts).astype(jnp.float32)
    frequency = rotary_base ** (-jnp.arange(0, ROT, 2, dtype=jnp.float32) / ROT)
    angles = positions[:, None] * frequency[None, :]
    return (jnp.cos(angles)[:, None, :], jnp.sin(angles)[:, None, :])


def rotate(field, cosines, sines, direction):
    half_rot = ROT // 2
    first_half = field[..., :half_rot]
    second = field[..., half_rot:ROT]
    return jnp.concatenate(
        [
            first_half * cosines - direction * second * sines,
            second * cosines + direction * first_half * sines,
            field[..., ROT:],
        ],
        -1,
    )


def score_block(query_block, keys_rot, seg_block, row_ids, segment_row, col_ids):
    scale = HEAD_DIM ** (-0.5)
    scores = (
        jnp.einsum("ihd,jhd->hij", query_block, keys_rot, preferred_element_type=jnp.float32)
        * scale
    )
    allowed = (seg_block[:, None] == segment_row[None, :]) & (row_ids[:, None] >= col_ids[None, :])
    return jnp.where(allowed[None], scores, masked_score)


def attention_forward(queries, keys_rot, values, segment_row):
    segment_length, heads_here, head_size = queries.shape
    block_rows = min(512, segment_length)
    block_count = segment_length // block_rows
    col_ids = jnp.arange(segment_length, dtype=jnp.int32)

    def one_block(packed):
        query_block, seg_block, row_ids = packed
        scores = score_block(query_block, keys_rot, seg_block, row_ids, segment_row, col_ids)
        row_max = jnp.max(scores, -1, keepdims=True)
        log_total = row_max[..., 0] + jnp.log(jnp.sum(jnp.exp(scores - row_max), -1))
        probability = jnp.exp(scores - log_total[..., None]).astype(jnp.bfloat16)
        attended = jnp.einsum(
            "hij,jhd->ihd", probability, values, preferred_element_type=jnp.float32
        ).astype(jnp.bfloat16)
        return (attended, log_total)

    attended, log_totals = lax.map(
        one_block,
        (
            queries.reshape(block_count, block_rows, heads_here, head_size),
            segment_row.reshape(block_count, block_rows),
            col_ids.reshape(block_count, block_rows),
        ),
    )
    return (attended.reshape(segment_length, heads_here, head_size), log_totals)


def attention_backward(queries, keys_rot, values, attended, log_totals, grad_att, segment_row):
    segment_length, heads_here, head_size = queries.shape
    block_rows = min(512, segment_length)
    block_count = segment_length // block_rows
    col_ids = jnp.arange(segment_length, dtype=jnp.int32)
    scale = HEAD_DIM ** (-0.5)

    def one_block(running, packed):
        grad_keys, grad_values = running
        query_block, out_block, grad_block, log_total, seg_block, row_ids = packed
        scores = score_block(query_block, keys_rot, seg_block, row_ids, segment_row, col_ids)
        probability = jnp.exp(scores - log_total[..., None])
        prob_low = probability.astype(jnp.bfloat16)
        delta = jnp.sum(grad_block.astype(jnp.float32) * out_block.astype(jnp.float32), -1).T
        grad_values = grad_values + jnp.einsum(
            "hij,ihd->jhd", prob_low, grad_block, preferred_element_type=jnp.float32
        )
        grad_prob = jnp.einsum(
            "ihd,jhd->hij", grad_block, values, preferred_element_type=jnp.float32
        )
        grad_scores = (probability * (grad_prob - delta[..., None]) * scale).astype(jnp.bfloat16)
        grad_query = jnp.einsum(
            "hij,jhd->ihd", grad_scores, keys_rot, preferred_element_type=jnp.float32
        )
        grad_keys = grad_keys + jnp.einsum(
            "hij,ihd->jhd", grad_scores, query_block, preferred_element_type=jnp.float32
        )
        return ((grad_keys, grad_values), grad_query)

    zero_field = jnp.zeros((segment_length, heads_here, head_size), jnp.float32)
    shaped = (
        queries.reshape(block_count, block_rows, heads_here, head_size),
        attended.reshape(block_count, block_rows, heads_here, head_size),
        grad_att.reshape(block_count, block_rows, heads_here, head_size),
        log_totals,
        segment_row.reshape(block_count, block_rows),
        col_ids.reshape(block_count, block_rows),
    )
    (grad_keys, grad_values), grad_query = lax.scan(one_block, (zero_field, zero_field), shaped)
    return (grad_query.reshape(segment_length, heads_here, head_size), grad_keys, grad_values)


def local_general(
    hidden_in,
    cotangent,
    segments,
    shared_params,
    split_params,
    shared_m1,
    split_m1,
    shared_m2,
    split_m2,
):
    tokens_here = hidden_in.shape[0]
    seq_count = lax.axis_size("seq")
    heads_here = HEADS // seq_count
    qkv_cols = 3 * MODEL_WIDTH // seq_count
    shared_full = lax.all_gather(shared_params, ("dp", "seq"), axis=0, tiled=True)
    b_qkv, b_dense, b_proj, gain_one, shift_one, gain_two, shift_two = unpack_shared(shared_full)
    split_mine = lax.all_gather(split_params.astype(jnp.bfloat16), "dp", axis=1, tiled=True)
    w_qkv_share, dense_weight, expand_weight, b_fc, contract_weight = unpack_split(
        split_mine, seq_count
    )
    b_fc = b_fc.astype(jnp.float32)
    column_rows = lax.all_gather(split_mine[:, : MODEL_WIDTH * qkv_cols], "seq", axis=0, tiled=True)
    w_qkv = (
        column_rows.reshape(seq_count, MODEL_WIDTH, qkv_cols)
        .transpose(1, 0, 2)
        .reshape(MODEL_WIDTH, 3 * MODEL_WIDTH)
    )
    resid = hidden_in.astype(jnp.float32)
    first_norm, normed_one, root_one = layer_norm(resid, gain_one, shift_one)
    second_norm, normed_two, root_two = layer_norm(resid, gain_two, shift_two)
    first_low = first_norm.astype(jnp.bfloat16)
    second_low = second_norm.astype(jnp.bfloat16)
    group_first, group_norm, group_cot = (
        lax.all_gather(first_low, "seq", axis=0, tiled=True),
        lax.all_gather(second_low, "seq", axis=0, tiled=True),
        lax.all_gather(cotangent, "seq", axis=0, tiled=True),
    )
    group_length = group_first.shape[0]
    qkv = (
        (jnp.dot(first_low, w_qkv, preferred_element_type=jnp.float32) + b_qkv)
        .astype(jnp.bfloat16)
        .reshape(tokens_here, HEADS, 3 * HEAD_DIM)
    )
    grouped = lax.all_to_all(qkv, "seq", split_axis=1, concat_axis=0, tiled=True)
    segment_row = segments[0]
    cosines, sines = rotary_tables(segment_row)
    queries = rotate(grouped[..., :HEAD_DIM].astype(jnp.float32), cosines, sines, 1.0).astype(
        jnp.bfloat16
    )
    keys_rot = rotate(
        grouped[..., HEAD_DIM : 2 * HEAD_DIM].astype(jnp.float32), cosines, sines, 1.0
    ).astype(jnp.bfloat16)
    values = grouped[..., 2 * HEAD_DIM :]
    attended, log_totals = attention_forward(queries, keys_rot, values, segment_row)
    grad_outf = cotangent.astype(jnp.float32)
    grad_b_proj = jnp.sum(grad_outf, 0)
    grad_b_dense = jnp.sum(grad_outf, 0)
    att_flat = attended.reshape(group_length, heads_here * HEAD_DIM)
    hidden_pre = jnp.dot(group_norm, expand_weight, preferred_element_type=jnp.float32) + b_fc
    hidden_activations = jax.nn.gelu(hidden_pre, approximate=False).astype(jnp.bfloat16)
    branch = jnp.dot(att_flat, dense_weight, preferred_element_type=jnp.float32) + jnp.dot(
        hidden_activations, contract_weight, preferred_element_type=jnp.float32
    )
    total = (
        resid + lax.psum_scatter(branch, "seq", scatter_dimension=0, tiled=True) + b_dense + b_proj
    )
    output = total.astype(jnp.bfloat16)
    grad_w_proj = jnp.dot(hidden_activations.T, group_cot, preferred_element_type=jnp.float32)
    grad_hidden = jnp.dot(
        group_cot, contract_weight.T, preferred_element_type=jnp.float32
    ) * gelu_slope(hidden_pre)
    grad_b_fc = jnp.sum(grad_hidden, 0)
    hidden_reduced_precision = grad_hidden.astype(jnp.bfloat16)
    grad_w_fc = jnp.dot(group_norm.T, hidden_reduced_precision, preferred_element_type=jnp.float32)
    grad_second = lax.psum_scatter(
        jnp.dot(hidden_reduced_precision, expand_weight.T, preferred_element_type=jnp.float32),
        "seq",
        scatter_dimension=0,
        tiled=True,
    )
    grad_w_dense = jnp.dot(att_flat.T, group_cot, preferred_element_type=jnp.float32)
    grad_att_heads = (
        jnp.dot(group_cot, dense_weight.T, preferred_element_type=jnp.float32)
        .astype(jnp.bfloat16)
        .reshape(group_length, heads_here, HEAD_DIM)
    )
    grad_query, grad_keys, grad_values = attention_backward(
        queries, keys_rot, values, attended, log_totals, grad_att_heads, segment_row
    )
    grad_query = rotate(grad_query, cosines, sines, -1.0)
    grad_keys = rotate(grad_keys, cosines, sines, -1.0)
    grad_grouped = jnp.concatenate([grad_query, grad_keys, grad_values], -1).astype(jnp.bfloat16)
    grad_w_qkv_share = jnp.dot(
        group_first.T,
        grad_grouped.reshape(group_length, qkv_cols),
        preferred_element_type=jnp.float32,
    )
    grad_qkv = lax.all_to_all(grad_grouped, "seq", split_axis=0, concat_axis=1, tiled=True).reshape(
        tokens_here, 3 * MODEL_WIDTH
    )
    grad_b_qkv = jnp.sum(grad_qkv.astype(jnp.float32), 0)
    grad_first = jnp.dot(grad_qkv, w_qkv.T, preferred_element_type=jnp.float32)
    grad_gain_one = jnp.sum(grad_first * normed_one, 0)
    grad_shift_one = jnp.sum(grad_first, 0)
    grad_gain_two = jnp.sum(grad_second * normed_two, 0)
    grad_shift_two = jnp.sum(grad_second, 0)
    input_grad = (
        grad_outf
        + norm_back(grad_first, gain_one, normed_one, root_one)
        + norm_back(grad_second, gain_two, normed_two, root_two)
    )
    shared_flat = jnp.concatenate(
        [
            grad_b_qkv,
            grad_b_dense,
            grad_b_proj,
            grad_gain_one,
            grad_shift_one,
            grad_gain_two,
            grad_shift_two,
        ]
    )
    shared_grads = lax.psum_scatter(shared_flat, ("dp", "seq"), scatter_dimension=0, tiled=True)
    split_local = pack_split(
        grad_w_qkv_share, grad_w_dense, grad_w_fc, grad_b_fc, grad_w_proj, seq_count
    )
    split_grads = lax.psum_scatter(split_local, "dp", scatter_dimension=1, tiled=True)
    shared_new, shared_m1_new, shared_m2_new = adamw(
        shared_params, shared_m1, shared_m2, shared_grads
    )
    split_new, split_m1_new, split_m2_new = adamw(split_params, split_m1, split_m2, split_grads)
    return (
        output,
        input_grad,
        shared_grads,
        split_grads,
        shared_new,
        split_new,
        shared_m1_new,
        split_m1_new,
        shared_m2_new,
        split_m2_new,
    )


LANES = 128


def share_layout(seq_count):
    ql = 3 * MODEL_WIDTH // seq_count
    dl = MODEL_WIDTH // seq_count
    fl = FF // seq_count
    return [
        MODEL_WIDTH * ql // LANES,
        dl * MODEL_WIDTH // LANES,
        MODEL_WIDTH * fl // LANES,
        fl // LANES,
        fl * MODEL_WIDTH // LANES,
    ]


Z = 4
DP = 2 * Z
SEQ = 4
BLOCK = 3072
EDGE = 16
SPAN = BLOCK + EDGE
MESH = pl.DeviceIdType.MESH
GATHER_CHUNKS = [(k * 768, 768) for k in range(4)]
REDUCE_CHUNKS = [(0, 784), (784, 768), (1552, 768), (2320, 768)]
SHARED_ROWS = 8
PLACE_ROWS = 256
STEP_ROWS = 448
SUM_ROWS = 7 * STEP_ROWS + EDGE


def enter(d, s):
    barrier = pltpu.get_barrier_semaphore()
    for k in range(1, DP):
        pl.semaphore_signal(
            barrier, inc=1, device_id=(lax.rem(d + k, DP), s), device_id_type=MESH
        )
    for k in range(1, SEQ):
        pl.semaphore_signal(
            barrier, inc=1, device_id=(d, lax.rem(s + k, SEQ)), device_id_type=MESH
        )
    pl.semaphore_wait(barrier, DP - 1 + SEQ - 1)


def remote(src, dst, send_sem, recv_sem, device):
    return pltpu.make_async_remote_copy(
        src_ref=src,
        dst_ref=dst,
        send_sem=send_sem,
        recv_sem=recv_sem,
        device_id=device,
        device_id_type=MESH,
    )


def gather_kernel(
    source, shared, full, shared_all, load, mine, placed, tails, row, send, recv_z, recv_x, s_send, s_recv, d_send, d_recv
):
    d, s = lax.axis_index("dp"), lax.axis_index("seq")
    z, x = d // 2, lax.rem(d, 2)
    parts = len(GATHER_CHUNKS) + 1
    fetch = pltpu.make_async_copy(source.at[:, 0, :], mine, load)
    fetch.start()
    fetch.wait()
    rows = mine.shape[0]
    edge = jnp.zeros((EDGE, LANES), jnp.float32)
    placed[:EDGE, :] = edge
    placed[BLOCK:, :] = edge
    for offset in range(0, rows, PLACE_ROWS):
        size = min(PLACE_ROWS, rows - offset)
        placed[pl.ds(d + offset, size), :] = mine[offset : offset + size, :]
    for offset in range(0, BLOCK, PLACE_ROWS):
        at = pl.multiple_of(d * BLOCK + offset, PLACE_ROWS)
        full[pl.ds(at, PLACE_ROWS), :] = placed[offset : offset + PLACE_ROWS, :].astype(full.dtype)
    tails[d] = placed[BLOCK:, :].astype(full.dtype)
    row[s] = shared[...]
    enter(d, s)

    def piece(zp, xp, c):
        if c == parts - 1:
            return tails.at[2 * zp + xp]
        offset, size = GATHER_CHUNKS[c]
        return full.at[pl.ds(pl.multiple_of((2 * zp + xp) * BLOCK + offset, 256), size)]

    def up(zp, c):
        ref = piece(zp, x, c)
        return remote(ref, ref, send.at[0, zp, c], recv_z.at[zp, c], (2 * (z + 1) + x, s))

    def down(zp, c):
        ref = piece(zp, x, c)
        return remote(ref, ref, send.at[1, zp, c], recv_z.at[zp, c], (2 * (z - 1) + x, s))

    def across(zp, c):
        ref = piece(zp, x, c)
        return remote(ref, ref, send.at[2, zp, c], recv_x.at[zp, c], (2 * z + 1 - x, s))

    def to_share(k):
        ref = row.at[s]
        return remote(ref, ref, s_send.at[k], s_recv.at[s], (d, lax.rem(s + k, SEQ)))

    def from_share(k):
        other = lax.rem(s + k, SEQ)
        ref = row.at[other]
        return remote(ref, ref, s_send.at[k], s_recv.at[other], (d, other))

    def to_group(k):
        return remote(
            row, shared_all.at[d], d_send.at[k], d_recv.at[d], (lax.rem(d + k, DP), s)
        )

    def from_group(k):
        other = lax.rem(d + k, DP)
        return remote(row, shared_all.at[other], d_send.at[k], d_recv.at[other], (other, s))

    for k in range(1, SEQ):
        to_share(k).start()
    for c in range(parts):
        pl.when(z < Z - 1)(lambda: up(z, c).start())
        pl.when(z > 0)(lambda: down(z, c).start())
        across(z, c).start()
    for k in range(1, SEQ):
        from_share(k).wait_recv()
    shared_all[d] = row[...]
    for k in range(1, DP):
        to_group(k).start()
    for k in range(1, Z):
        for c in range(parts):

            @pl.when(z >= k)
            def _():
                up(z - k, c).wait_recv()
                pl.when(z < Z - 1)(lambda: up(z - k, c).start())
                across(z - k, c).start()

            @pl.when(z + k < Z)
            def _():
                down(z + k, c).wait_recv()
                pl.when(z > 0)(lambda: down(z + k, c).start())
                across(z + k, c).start()

    for zp in range(Z):
        for c in range(parts):
            ref = piece(zp, 1 - x, c)
            remote(
                ref, ref, send.at[2, zp, c], recv_x.at[zp, c], (2 * z + 1 - x, s)
            ).wait_recv()
            across(zp, c).wait_send()
            pl.when((z >= zp) & (z < Z - 1))(lambda: up(zp, c).wait_send())
            pl.when((z <= zp) & (z > 0))(lambda: down(zp, c).wait_send())
    for k in range(1, SEQ):
        to_share(k).wait_send()
    for k in range(1, DP):
        to_group(k).wait_send()
        from_group(k).wait_recv()
    for k in range(1, DP):
        head = full[k * BLOCK : k * BLOCK + EDGE, :].astype(jnp.float32)
        tail = tails[k - 1].astype(jnp.float32)
        full[k * BLOCK : k * BLOCK + EDGE, :] = (head + tail).astype(jnp.bfloat16)
    full[DP * BLOCK :, :] = tails[DP - 1]


def gather_parts(split_params, shared_params, dp_count, seq_count):
    rows = split_params.shape[1] // LANES
    mine = split_params.reshape(rows, 1, LANES)
    count = shared_params.shape[0]
    padded = jnp.pad(shared_params, (0, SHARED_ROWS * LANES - count))
    vmem = pl.BlockSpec(memory_space=pltpu.VMEM)
    parts = len(GATHER_CHUNKS) + 1
    dma = pltpu.SemaphoreType.DMA
    full, shared_all = pl.pallas_call(
        gather_kernel,
        out_shape=(
            jax.ShapeDtypeStruct((DP * BLOCK + EDGE, LANES), jnp.bfloat16),
            jax.ShapeDtypeStruct((DP, SEQ, SHARED_ROWS, LANES), jnp.float32),
        ),
        in_specs=[pl.BlockSpec(memory_space=pl.ANY), vmem],
        out_specs=(vmem, vmem),
        scratch_shapes=[
            dma,
            pltpu.VMEM((rows, LANES), jnp.float32),
            pltpu.VMEM((SPAN, LANES), jnp.float32),
            pltpu.VMEM((DP, EDGE, LANES), jnp.bfloat16),
            pltpu.VMEM((SEQ, SHARED_ROWS, LANES), jnp.float32),
            dma((3, Z, parts)),
            dma((Z, parts)),
            dma((Z, parts)),
            dma((SEQ,)),
            dma((SEQ,)),
            dma((DP,)),
            dma((DP,)),
        ],
        compiler_params=pltpu.CompilerParams(
            collective_id=0, has_side_effects=True, vmem_limit_bytes=24 * 2**20
        ),
        cost_estimate=pl.CostEstimate(flops=0, bytes_accessed=200 * 2**20, transcendentals=0),
        name="gather_params",
    )(mine, padded.reshape(SHARED_ROWS, LANES))
    shared_full = shared_all.reshape(DP * SEQ, SHARED_ROWS * LANES)[:, :count].reshape(-1)
    return full, shared_full


def reduce_kernel(
    flat,
    shared,
    out,
    shared_out,
    x_in,
    up_in,
    down_in,
    stage,
    share_in,
    share_sum,
    group_in,
    x_send,
    x_recv,
    z_send,
    up_recv,
    down_recv,
    s_send,
    s_recv,
    d_send,
    d_recv,
):
    d, s = lax.axis_index("dp"), lax.axis_index("seq")
    z, x = d // 2, lax.rem(d, 2)
    f32 = jnp.float32
    enter(d, s)

    def across(zp, c):
        offset, size = REDUCE_CHUNKS[c]
        start = pl.multiple_of((2 * zp + 1 - x) * BLOCK + offset, EDGE)
        return remote(
            flat.at[pl.ds(start, size)],
            x_in.at[zp, pl.ds(offset, size)],
            x_send.at[zp, c],
            x_recv.at[zp, c],
            (2 * z + 1 - x, s),
        )

    def along(zp, c, step, into, recv):
        offset, size = REDUCE_CHUNKS[c]
        return remote(
            stage.at[zp, pl.ds(offset, size)],
            into.at[zp, pl.ds(offset, size)],
            z_send.at[zp, c],
            recv.at[zp, c],
            (2 * (z + step) + x, s),
        )

    def up(zp, c):
        return along(zp, c, 1, up_in, up_recv)

    def down(zp, c):
        return along(zp, c, -1, down_in, down_recv)

    def add(zp, c, others, store):
        offset, size = REDUCE_CHUNKS[c]
        tile = 112 if size % 128 else 128

        def body(k, carry):
            at = pl.multiple_of(offset + k * tile, EDGE)
            own = pl.multiple_of((2 * zp + x) * BLOCK + offset + k * tile, EDGE)
            total = flat[pl.ds(own, tile), :].astype(f32)
            for ref in (x_in, *others):
                total = total + ref[zp, pl.ds(at, tile), :].astype(f32)
            store(at, tile, total)
            return carry

        lax.fori_loop(0, size // tile, body, 0)

    def hop(zp, c, others, copy):
        def store(at, tile, total):
            stage[zp, pl.ds(at, tile), :] = total.astype(jnp.bfloat16)

        add(zp, c, others, store)
        copy.start()

    def to_share(k):
        other = lax.rem(s + k, SEQ)
        return remote(
            shared.at[other], share_in.at[s], s_send.at[k], s_recv.at[s], (d, other)
        )

    def from_share(k):
        other = lax.rem(s + k, SEQ)
        return remote(
            shared.at[s], share_in.at[other], s_send.at[k], s_recv.at[other], (d, other)
        )

    def to_group(k):
        other = lax.rem(d + k, DP)
        return remote(
            share_sum.at[other], group_in.at[d], d_send.at[k], d_recv.at[d], (other, s)
        )

    def from_group(k):
        other = lax.rem(d + k, DP)
        return remote(
            share_sum.at[d], group_in.at[other], d_send.at[k], d_recv.at[other], (other, s)
        )

    chunks = range(len(REDUCE_CHUNKS))
    items = [(zp, c) for c in chunks for zp in (Z - 1, 0)]
    items += [(zp, c) for c in chunks for zp in (2, 1)]
    ahead = 6
    for k in range(1, SEQ):
        to_share(k).start()
    for zp, c in items[:ahead]:
        across(zp, c).start()
    share_in[s] = shared[s]
    for k in range(1, SEQ):
        from_share(k).wait_recv()
    share_sum[...] = share_in[0] + share_in[1] + share_in[2] + share_in[3]
    for k in range(1, DP):
        to_group(k).start()
    group_in[d] = share_sum[d]

    for t, (zp, c) in enumerate(items):
        if t + ahead < len(items):
            across(*items[t + ahead]).start()

        @pl.when(z != zp)
        def _():
            across(zp, c).wait_recv()

        if zp > 0:

            @pl.when(z == 0)
            def _():
                hop(zp, c, (), up(zp, c))

        if zp > 1:

            @pl.when((z > 0) & (z < zp))
            def _():
                up(zp, c).wait_recv()
                hop(zp, c, (up_in,), up(zp, c))

        if zp < Z - 1:

            @pl.when(z == Z - 1)
            def _():
                hop(zp, c, (), down(zp, c))

        if zp < Z - 2:

            @pl.when((z < Z - 1) & (z > zp))
            def _():
                down(zp, c).wait_recv()
                hop(zp, c, (down_in,), down(zp, c))

    def keep(at, tile, total):
        out[pl.ds(at, tile), :] = total

    out[SPAN:, :] = jnp.zeros((SUM_ROWS - SPAN, LANES), f32)
    for c in chunks:
        across(z, c).wait_recv()

        @pl.when(z == 0)
        def _():
            down(z, c).wait_recv()
            add(z, c, (down_in,), keep)

        @pl.when(z == Z - 1)
        def _():
            up(z, c).wait_recv()
            add(z, c, (up_in,), keep)

        @pl.when((z > 0) & (z < Z - 1))
        def _():
            up(z, c).wait_recv()
            down(z, c).wait_recv()
            add(z, c, (up_in, down_in), keep)

    for zp, c in items:
        across(zp, c).wait_send()
        pl.when(z < zp)(lambda: up(zp, c).wait_send())
        pl.when(z > zp)(lambda: down(zp, c).wait_send())
    for k in range(1, SEQ):
        to_share(k).wait_send()
    for k in range(1, DP):
        to_group(k).wait_send()
        from_group(k).wait_recv()
    total = group_in[0]
    for k in range(1, DP):
        total = total + group_in[k]
    shared_out[...] = total


def reduce_parts(flat, shared_flat, dp_count, seq_count):
    count = shared_flat.shape[0] // (DP * SEQ)
    flat = jnp.pad(flat, ((0, DP * BLOCK + EDGE - flat.shape[0]), (0, 0)))
    shared = jnp.pad(
        shared_flat.reshape(DP, SEQ, count), ((0, 0), (0, 0), (0, SHARED_ROWS * LANES - count))
    )
    shared = shared.transpose(1, 0, 2).reshape(SEQ, DP, SHARED_ROWS, LANES)
    vmem = pl.BlockSpec(memory_space=pltpu.VMEM)
    dma = pltpu.SemaphoreType.DMA
    held = pltpu.VMEM((Z, SPAN, LANES), jnp.bfloat16)
    sems = dma((Z, len(REDUCE_CHUNKS)))
    out, shared_out = pl.pallas_call(
        reduce_kernel,
        out_shape=(
            jax.ShapeDtypeStruct((SUM_ROWS, LANES), jnp.float32),
            jax.ShapeDtypeStruct((SHARED_ROWS, LANES), jnp.float32),
        ),
        in_specs=[vmem, vmem],
        out_specs=(vmem, vmem),
        scratch_shapes=[
            held,
            held,
            held,
            held,
            pltpu.VMEM((SEQ, DP, SHARED_ROWS, LANES), jnp.float32),
            pltpu.VMEM((DP, SHARED_ROWS, LANES), jnp.float32),
            pltpu.VMEM((DP, SHARED_ROWS, LANES), jnp.float32),
            sems,
            sems,
            sems,
            sems,
            sems,
            dma((SEQ,)),
            dma((SEQ,)),
            dma((DP,)),
            dma((DP,)),
        ],
        compiler_params=pltpu.CompilerParams(
            collective_id=1, has_side_effects=True, vmem_limit_bytes=40 * 2**20
        ),
        cost_estimate=pl.CostEstimate(flops=0, bytes_accessed=250 * 2**20, transcendentals=0),
        name="reduce_grads",
    )(flat, shared)
    return out, shared_out.reshape(-1)[:count]


def adamw_kernel(where, sums, *refs):
    sources, targets, held, results = refs[:3], refs[3:7], refs[7:10], refs[10:14]
    load, store = refs[14:]
    rows = held[0].shape[0]
    loads = [
        pltpu.make_async_copy(ref.at[:, 0, :], part, load.at[k])
        for k, (ref, part) in enumerate(zip(sources, held))
    ]
    for copy in loads:
        copy.start()
    for copy in loads:
        copy.wait()
    starts = list(range(0, rows, STEP_ROWS))
    stores = []
    for t, offset in enumerate(starts):
        size = min(STEP_ROWS, rows - offset)
        at = slice(offset, offset + size)
        grads = sums[pl.ds(where[0] + offset, size), :]
        values = (grads, *adamw(*(part[at, :] for part in held), grads))
        for k, value in enumerate(values):
            results[k][at, :] = value
            copy = pltpu.make_async_copy(
                results[k].at[at, :], targets[k].at[at, 0, :], store.at[k, t]
            )
            copy.start()
            stores.append(copy)
    for copy in stores:
        copy.wait()


def adamw_rows(sums, params, first_m, second_m):
    shape = params.shape
    rows = shape[1] // LANES
    hbm = pl.BlockSpec(memory_space=pl.ANY)
    dma = pltpu.SemaphoreType.DMA
    results = pl.pallas_call(
        adamw_kernel,
        out_shape=[jax.ShapeDtypeStruct((rows, 1, LANES), jnp.float32)] * 4,
        in_specs=[
            pl.BlockSpec(memory_space=pltpu.SMEM),
            pl.BlockSpec(memory_space=pltpu.VMEM),
            hbm,
            hbm,
            hbm,
        ],
        out_specs=[hbm] * 4,
        scratch_shapes=[pltpu.VMEM((rows, LANES), jnp.float32)] * 7
        + [dma((3,)), dma((4, pl.cdiv(rows, STEP_ROWS)))],
        compiler_params=pltpu.CompilerParams(vmem_limit_bytes=24 * 2**20),
        name="adamw_rows",
    )(
        lax.axis_index("dp").reshape(1),
        sums,
        *(part.reshape(rows, 1, LANES) for part in (params, first_m, second_m)),
    )
    return [part.reshape(shape) for part in results]


def attend(queries, keys_rot, values, segment_row):
    length = queries.shape[1]
    ids = jnp.arange(length, dtype=jnp.int32)
    allowed = (segment_row[:, None] == segment_row[None, :]) & (ids[:, None] >= ids[None, :])
    scores = jnp.einsum("hid,hjd->hij", queries, keys_rot, preferred_element_type=jnp.float32)
    scores = jnp.where(allowed[None], scores * HEAD_DIM ** (-0.5), masked_score)
    row_max = jnp.max(scores, -1, keepdims=True)
    log_total = row_max + jnp.log(jnp.sum(jnp.exp(scores - row_max), -1, keepdims=True))
    prob = jnp.exp(scores - log_total)
    prob_low = prob.astype(jnp.bfloat16)
    attended = jnp.einsum("hij,hjd->hid", prob_low, values, preferred_element_type=jnp.float32)
    return attended.astype(jnp.bfloat16), prob, prob_low


def attend_back(queries, keys_rot, values, attended, prob, prob_low, grad_att):
    delta = jnp.sum(grad_att.astype(jnp.float32) * attended.astype(jnp.float32), -1, keepdims=True)
    grad_values = jnp.einsum("hij,hid->hjd", prob_low, grad_att, preferred_element_type=jnp.float32)
    grad_prob = jnp.einsum("hid,hjd->hij", grad_att, values, preferred_element_type=jnp.float32)
    grad_scores = (prob * (grad_prob - delta) * HEAD_DIM ** (-0.5)).astype(jnp.bfloat16)
    grad_query = jnp.einsum(
        "hij,hjd->hid", grad_scores, keys_rot, preferred_element_type=jnp.float32
    )
    grad_keys = jnp.einsum("hij,hid->hjd", grad_scores, queries, preferred_element_type=jnp.float32)
    return grad_query, grad_keys, grad_values


def local_grouped(
    hidden_in,
    cotangent,
    segments,
    shared_params,
    split_params,
    shared_m1,
    split_m1,
    shared_m2,
    split_m2,
):
    dp_count = lax.axis_size("dp")
    seq_count = lax.axis_size("seq")
    share = lax.axis_index("seq")
    heads_here = HEADS // seq_count
    ql = 3 * MODEL_WIDTH // seq_count
    dl = MODEL_WIDTH // seq_count
    fl = FF // seq_count
    f32, bf16 = jnp.float32, jnp.bfloat16
    tokens_here = hidden_in.shape[0]
    both = lax.all_gather(
        jnp.concatenate([hidden_in, cotangent], 1), "seq", axis=0, tiled=True
    )
    group_hidden, group_cot = both[:, :MODEL_WIDTH], both[:, MODEL_WIDTH:]
    full, shared_full = gather_parts(split_params, shared_params, dp_count, seq_count)
    b_qkv, b_dense, b_proj, gain_one, shift_one, gain_two, shift_two = unpack_shared(shared_full)
    extents = share_layout(seq_count)
    offsets = [sum(extents[:k]) for k in range(6)]
    w_qkv, w_dense, w_fc, b_fc, w_proj = [
        full[offsets[k] : offsets[k + 1]].reshape(shape)
        for k, shape in enumerate(
            [(MODEL_WIDTH, ql), (dl, MODEL_WIDTH), (MODEL_WIDTH, fl), (fl,), (fl, MODEL_WIDTH)]
        )
    ]
    b_fc = b_fc.astype(f32)
    b_qkv_mine = lax.dynamic_slice(b_qkv, (share * ql,), (ql,))

    resid = group_hidden.astype(f32)
    first_norm, normed, root = layer_norm(resid, gain_one, shift_one)
    first_low = first_norm.astype(bf16)
    second_low = (normed * gain_two + shift_two).astype(bf16)
    length = resid.shape[0]

    qkv = (jnp.dot(first_low, w_qkv, preferred_element_type=f32) + b_qkv_mine).astype(bf16)
    qkv = qkv.reshape(length, heads_here, 3, HEAD_DIM).transpose(2, 1, 0, 3)
    segment_row = segments[0]
    cosines, sines = rotary_tables(segment_row)
    cosines, sines = cosines[:, 0], sines[:, 0]
    queries = rotate(qkv[0].astype(f32), cosines, sines, 1.0).astype(bf16)
    keys_rot = rotate(qkv[1].astype(f32), cosines, sines, 1.0).astype(bf16)
    values = qkv[2]
    attended, prob, prob_low = attend(queries, keys_rot, values, segment_row)
    att_flat = attended.transpose(1, 0, 2).reshape(length, dl)

    hidden_pre = jnp.dot(second_low, w_fc, preferred_element_type=f32) + b_fc
    activated = jax.nn.gelu(hidden_pre, approximate=False).astype(bf16)
    branch = jnp.dot(att_flat, w_dense, preferred_element_type=f32) + jnp.dot(
        activated, w_proj, preferred_element_type=f32
    )
    total = lax.psum_scatter(branch, "seq", scatter_dimension=0, tiled=True)
    output = (hidden_in.astype(f32) + total + b_dense + b_proj).astype(bf16)

    grad_outf = cotangent.astype(f32)
    grad_b_out = jnp.sum(grad_outf, 0)
    grad_w_proj = jnp.dot(activated.T, group_cot, preferred_element_type=f32)
    grad_hidden = jnp.dot(group_cot, w_proj.T, preferred_element_type=f32) * gelu_slope(hidden_pre)
    grad_b_fc = jnp.sum(grad_hidden, 0)
    grad_hidden_low = grad_hidden.astype(bf16)
    grad_w_fc = jnp.dot(second_low.T, grad_hidden_low, preferred_element_type=f32)
    grad_second = jnp.dot(grad_hidden_low, w_fc.T, preferred_element_type=f32)
    grad_w_dense = jnp.dot(att_flat.T, group_cot, preferred_element_type=f32)
    grad_att = (
        jnp.dot(group_cot, w_dense.T, preferred_element_type=f32)
        .astype(bf16)
        .reshape(length, heads_here, HEAD_DIM)
        .transpose(1, 0, 2)
    )
    grad_query, grad_keys, grad_values = attend_back(
        queries, keys_rot, values, attended, prob, prob_low, grad_att
    )
    grad_query = rotate(grad_query, cosines, sines, -1.0)
    grad_keys = rotate(grad_keys, cosines, sines, -1.0)
    grad_qkv = (
        jnp.stack([grad_query, grad_keys, grad_values])
        .astype(bf16)
        .transpose(2, 1, 0, 3)
        .reshape(length, ql)
    )
    grad_b_qkv = jnp.sum(grad_qkv.astype(f32), 0)
    grad_w_qkv = jnp.dot(first_low.T, grad_qkv, preferred_element_type=f32)
    grad_first = jnp.dot(grad_qkv, w_qkv.T, preferred_element_type=f32)

    scaled = lax.psum_scatter(
        gain_one * grad_first + gain_two * grad_second, "seq", scatter_dimension=0, tiled=True
    )
    normed_mine = lax.dynamic_slice(normed, (share * tokens_here, 0), (tokens_here, MODEL_WIDTH))
    root_mine = lax.dynamic_slice(root, (share * tokens_here, 0), (tokens_here, 1))
    input_grad = grad_outf + norm_back(scaled, 1.0, normed_mine, root_mine)

    shared_flat = jnp.concatenate(
        [
            lax.dynamic_update_slice(
                jnp.zeros((3 * MODEL_WIDTH,), f32), grad_b_qkv, (share * ql,)
            ),
            grad_b_out,
            grad_b_out,
            jnp.sum(grad_first * normed, 0),
            jnp.sum(grad_first, 0),
            jnp.sum(grad_second * normed, 0),
            jnp.sum(grad_second, 0),
        ]
    )
    flat = jnp.concatenate(
        [
            part.astype(bf16).reshape(-1, LANES)
            for part in (grad_w_qkv, grad_w_dense, grad_w_fc, grad_b_fc, grad_w_proj)
        ]
    )
    split_sums, shared_grads = reduce_parts(flat, shared_flat, dp_count, seq_count)
    shared_new, shared_m1_new, shared_m2_new = adamw(
        shared_params, shared_m1, shared_m2, shared_grads
    )
    split_grads, split_new, split_m1_new, split_m2_new = adamw_rows(
        split_sums, split_params, split_m1, split_m2
    )
    return (
        output,
        input_grad,
        shared_grads,
        split_grads,
        shared_new,
        split_new,
        shared_m1_new,
        split_m1_new,
        shared_m2_new,
        split_m2_new,
    )


def solution(mesh):
    in_specs = (
        P(("dp", "seq"), None),
        P(("dp", "seq"), None),
        P("dp", None),
        P(("dp", "seq")),
        P("seq", "dp"),
        P(("dp", "seq")),
        P("seq", "dp"),
        P(("dp", "seq")),
        P("seq", "dp"),
    )
    out_specs = (
        P(("dp", "seq"), None),
        P(("dp", "seq"), None),
        P(("dp", "seq")),
        P("seq", "dp"),
        P(("dp", "seq")),
        P("seq", "dp"),
        P(("dp", "seq")),
        P("seq", "dp"),
        P(("dp", "seq")),
        P("seq", "dp"),
    )
    dp_count, seq_count = mesh.shape["dp"], mesh.shape["seq"]
    local = local_grouped if (dp_count, seq_count) == (DP, SEQ) else local_general
    return jax.shard_map(local, mesh=mesh, in_specs=in_specs, out_specs=out_specs, check_vma=False)
```

profile of v0, /device:TPU:0, one launch (start us, length us, event | category | flops | bytes accessed | tf_op | source)
XLA Modules:
  0.0 281.4 jit_solution(2450248791152042972)
XLA Ops:
  7.2 2.0 pad_maximum_fusion
  9.3 0.7 pad_bitcast_fusion.1.shared
  10.0 77.6 %gather_params.1 = (bf16[24592,128]{1,0:T(8,128)(2,1)S(1)}, f32[8,4,8,128]{3,2,1,0:T(8,128)S(1)}) custom-call(f32[3073,1,128]{2,1,0:T(1,128)S(1)} %bitcast.89, f32[8,128]{1,0:T(8,128)S(1)} %pad_bitcast_fusion.1.shared), custom_call_target="tpu_custom_call" | custom-call | bytes 209715200 | tf_op jit(solution)/shard_map/gather_params/pallas_call | solution.py:548
  87.6 0.9 slice.131
  88.5 0.1 slice.116
  88.6 2.7 fusion.44
  91.3 0.3 copy-done.2
  91.6 4.3 %reshape.313 = bf16[1024,1024]{1,0:T(8,128)(2,1)} reshape(bf16[8192,128]{1,0:T(8,128)(2,1)} %get-tuple-element.39) | data formatting | bytes 4194304 | tf_op jit(solution)/shard_map/reshape | solution.py:927
  95.9 0.1 reshape.307
  96.0 4.2 %reshape.314 = bf16[1024,1024]{1,0:T(8,128)(2,1)} reshape(bf16[8192,128]{1,0:T(8,128)(2,1)} %get-tuple-element.38) | data formatting | bytes 4194304 | tf_op jit(solution)/shard_map/reshape | solution.py:927
  100.2 2.1 reshape.312
  102.3 2.2 reshape.308
  104.7 0.3 reduce-window.9
  105.2 0.1 slice_reduce_fusion
  105.4 0.7 bitcast_convert_fusion
  106.1 0.1 broadcast_multiply_fusion
  106.2 0.2 fusion.21
  106.5 1.6 convert_reduce_fusion
  108.1 1.6 fusion.4
  109.7 2.5 add_convert_fusion.2
  112.3 0.3 copy.34
  112.6 0.2 fusion.37
  112.9 0.9 fusion.1
  113.8 0.9 exponential_reduce_fusion
  114.8 0.7 copy-done.9
  115.6 0.5 convolution_convert_fusion.6
  116.1 1.3 multiply_reduce_fusion.3
  117.4 1.3 fusion.20
  118.6 1.6 multiply_convert_fusion
  120.3 0.5 fusion.29
  120.8 0.7 fusion.31
  121.7 0.2 convert_reduce_fusion.1
  121.9 1.1 copy-done.14
  123.0 1.0 fusion.48
  124.1 0.6 copy-done.12
  124.6 6.9 %fusion.7 = (bf16[512,1024]{1,0:T(8,128)(2,1)}, f32[512,1024]{1,0:T(8,128)S(1)}) fusion(f32[1024]{0:T(1024)S(1)} %bitcast_convert_fusion, bf16[1024,1024]{1,0:T(8,128)(2,1)S(1)} %copy-done.12, f32[1024]{0:T(1024)S(1)} %get-tuple-element.58, f32[1024]{0:T(1024)S(1)} %get-tuple-element.59, f32[512]{0:T(512)S(1)} %add_rsqrt_fusion, ...), kind=kOutput, calls=%fused_computation.15 | convolution fusion | flops 1111490560 | bytes 6307840 | tf_op jit(solution)/shard_map/dot_general | solution.py:952
  131.5 2.1 fusion.46
  133.7 3.8 %multiply_reduce_fusion = (f32[1024]{0:T(1024)S(1)}, f32[1024]{0:T(1024)S(1)}, f32[1024]{0:T(1024)S(1)}, f32[1024]{0:T(1024)S(1)}, f32[512,1024]{1,0:T(8,128)}, /*index=5*/f32[512,1024]{1,0:T(8,128)}) fusion(f32[512]{0:T(512)S(1)} %add_rsqrt_fusion, f32[512]{0:T(512)S(1)} %broadcast_multiply_fusion.1, bf16[512,2048]{1,0:T(8,128)(2,1)S(1)} %copy-done.9, ...), kind=kOutput, calls=%fused_computation.21 | convolution fusion | flops 1080029184 | bytes 10514432 | tf_op jit(solution)/shard_map/dot_general | solution.py:967
  137.6 3.6 %convolution_convert_fusion.2 = bf16[1024,768]{1,0:T(8,128)(2,1)} fusion(bf16[512,768]{0,1:T(8,128)(2,1)S(1)} %bitcast.100, f32[1024]{0:T(1024)S(1)} %get-tuple-element.60, f32[1024]{0:T(1024)S(1)} %get-tuple-element.61, f32[512]{0:T(512)S(1)} %add_rsqrt_fusion, f32[512]{0:T(512)S(1)} %broadcast_multiply_fusion.1, ...), kind=kOutput, calls=%fused_computation.43 | convolution fusion | flops 809238528 | bytes 3420160 | tf_op jit(solution)/shard_map/dot_general | solution.py:987
  141.2 3.1 %reshape.317 = bf16[6144,128]{1,0:T(8,128)(2,1)S(1)} reshape(bf16[1024,768]{1,0:T(8,128)(2,1)} %convolution_convert_fusion.2) | data formatting | bytes 3145728 | tf_op jit(solution)/shard_map/reshape | solution.py:1012
  144.3 2.5 convolution_convert_fusion.3
  146.8 2.1 reshape.318
  148.9 3.2 %fusion.47 = f32[512,1024]{1,0:T(8,128)S(1)} fusion(bf16[512,1024]{1,0:T(8,128)(2,1)} %get-tuple-element.69, bf16[1024,1024]{1,0:T(8,128)(2,1)} %reshape.314), kind=kOutput, calls=%fused_computation.134 | convolution fusion | flops 1073741824 | bytes 5242880 | tf_op jit(solution)/shard_map/dot_general | solution.py:954
  152.1 1.8 convolution_add_fusion
  153.9 1.3 constant_dynamic-update-slice_fusion.4
  155.3 1.2 copy-done.22
  156.5 4.1 %convolution_convert_fusion.1 = bf16[1024,1024]{1,0:T(8,128)(2,1)} fusion(bf16[512,1024]{1,0:T(8,128)(2,1)S(1)} %copy-done.22, f32[1024]{0:T(1024)S(1)} %get-tuple-element.58, f32[1024]{0:T(1024)S(1)} %get-tuple-element.59, f32[512]{0:T(512)S(1)} %add_rsqrt_fusion, f32[512]{0:T(512)S(1)} %broadcast_multiply_fusion.1, ...), kind=kOutput, calls=%fused_computation.42 | convolution fusion | flops 1077936128 | bytes 4206592 | tf_op jit(solution)/shard_map/dot_general | solution.py:966
  160.6 2.7 convolution_convert_fusion
  163.3 0.9 constant_dynamic-update-slice_fusion.3
  164.3 4.2 %reshape.319 = bf16[8192,128]{1,0:T(8,128)(2,1)} reshape(bf16[1024,1024]{1,0:T(8,128)(2,1)} %convolution_convert_fusion.1) | data formatting | bytes 4194304 | tf_op jit(solution)/shard_map/reshape | solution.py:1012
  168.5 4.2 %reshape.320 = bf16[8192,128]{1,0:T(8,128)(2,1)} reshape(bf16[1024,1024]{1,0:T(8,128)(2,1)} %convolution_convert_fusion) | data formatting | bytes 4194304 | tf_op jit(solution)/shard_map/reshape | solution.py:1012
  172.7 3.2 %constant_dynamic-update-slice_fusion.2 = bf16[24584,128]{1,0:T(8,128)(2,1)} fusion(bf16[24584,128]{1,0:T(8,128)(2,1)} %constant_dynamic-update-slice_fusion.3, bf16[8192,128]{1,0:T(8,128)(2,1)} %reshape.319), kind=kLoop, calls=%fused_computation.95 | loop fusion | bytes 4194304
  175.9 0.6 constant_dynamic-update-slice_fusion.1
  176.5 1.6 constant_dynamic-update-slice_fusion
  178.1 6.0 %pad.13.flat = bf16[24592,128]{1,0:T(8,128)(2,1)} pad(bf16[24584,128]{1,0:T(8,128)(2,1)} %constant_dynamic-update-slice_fusion, bf16[]{:T(256)} %constant.58.clone.1), padding=0_8x0_0 | pad | bytes 12589058 | tf_op jit(solution)/shard_map/jit(_pad)/pad | solution.py:770
  184.1 0.2 dynamic_update_slice.3
  184.3 1.3 fusion.42
  185.7 2.2 convert_reduce_fusion.2
  187.9 0.1 reshape.321
  188.1 2.8 copy-done
  190.9 78.0 %reduce_grads.1 = (f32[3152,128]{1,0:T(8,128)S(1)}, f32[8,128]{1,0:T(8,128)S(1)}) custom-call(bf16[24592,128]{1,0:T(8,128)(2,1)S(1)} %copy-done, f32[4,8,8,128]{3,2,1,0:T(8,128)S(1)} %copy.49.shared), custom_call_target="tpu_custom_call" | custom-call | bytes 262144000 | tf_op jit(solution)/shard_map/reduce_grads/pallas_call | solution.py:779
  269.0 3.4 %adamw_rows.1 = (f32[3073,1,128]{2,1,0:T(1,128)}, f32[3073,1,128]{2,1,0:T(1,128)}, f32[3073,1,128]{2,1,0:T(1,128)}, f32[3073,1,128]{2,1,0:T(1,128)}) custom-call(s32[1]{0:T(128)} %bitcast.25.where, f32[3152,128]{1,0:T(8,128)S(1)} %get-tuple-element.21.sums, f32[3073,1,128]{2,1,0:T(1,128)S(1)} %bitcast.90, f32[3073,1,128]{2,1,0:T(1,128)S(1)} %bitcast.91, ...), custom_call_target="tpu_custom_call" | custom-call | tf_op jit(solution)/shard_map/adamw_rows/pallas_call | solution.py:849
  272.5 0.6 multiply_subtract_fusion
  273.1 1.8 add_convert_fusion.3
  (90 shorter events, 1.5 us)
Async XLA Ops:
  7.2 2.8 copy-start.1
  7.2 99.3 %all-gather.2.cloned.1.call-start = ((), (), s32[]{:S(2)}) async-start(), calls=%async_computation.2 | async-start | bytes 2621440 | tf_op jit(solution)/shard_map/all_gather | solution.py:918
  9.2 175.1 %reduce-scatter.5.cloned.1.call-start = ((), (), s32[]{:S(2)}) async-start(), calls=%async_computation.4 | async-start | bytes 2621440 | tf_op jit(solution)/shard_map/reduce_scatter | solution.py:990
  87.5 4.0 %copy-start.2 = (bf16[24592,128]{1,0:T(8,128)(2,1)}, bf16[24592,128]{1,0:T(8,128)(2,1)S(1)}, u32[]{:S(2)}) copy-start(bf16[24592,128]{1,0:T(8,128)(2,1)S(1)} %get-tuple-element.19) | copy-start | bytes 18886660
  100.2 4.3 %copy-start.17 = (s32[1,512]{1,0:T(1,128)S(1)}, s32[1,512]{1,0:T(1,128)}, u32[]{:S(2)}) copy-start(s32[1,512]{1,0:T(1,128)} %param.11) | copy-start | bytes 6148
  106.5 3.3 %copy-start.8 = (bf16[512,2048]{1,0:T(8,128)(2,1)S(1)}, bf16[512,2048]{1,0:T(8,128)(2,1)}, u32[]{:S(2)}) copy-start(bf16[512,2048]{1,0:T(8,128)(2,1)} %all-gather.2.cloned.1.call-done) | copy-start | bytes 6291460
  113.8 1.0 copy-start.6
  113.8 1.8 copy-start.9
  121.6 1.4 copy-start.14
  123.0 1.6 copy-start.12
  124.6 6.9 %copy-start.11 = (bf16[1024,1024]{1,0:T(8,128)(2,1)S(1)}, bf16[1024,1024]{1,0:T(8,128)(2,1)}, u32[]{:S(2)}) copy-start(bf16[1024,1024]{1,0:T(8,128)(2,1)} %reshape.314) | copy-start | bytes 6291460
  133.6 3.8 %copy-start.21 = (bf16[512,1024]{1,0:T(8,128)(2,1)}, bf16[512,1024]{1,0:T(8,128)(2,1)S(1)}, u32[]{:S(2)}) copy-start(bf16[512,1024]{1,0:T(8,128)(2,1)S(1)} %get-tuple-element.76) | copy-start | bytes 3145732
  137.5 135.6 %reduce-scatter.3.cloned.1.call-start = ((), (), s32[]{:S(2)}) async-start(), calls=%async_computation.3 | async-start | bytes 2621440 | tf_op jit(solution)/shard_map/reduce_scatter | solution.py:957
  148.9 3.2 %copy-start.7 = (bf16[256,1024]{1,0:T(8,128)(2,1)S(1)}, bf16[256,1024]{1,0:T(8,128)(2,1)}, u32[]{:S(2)}) copy-start(bf16[256,1024]{1,0:T(8,128)(2,1)} %reshape.312) | copy-start | bytes 1572868
  155.2 1.2 copy-start.22
  156.5 4.2 %copy-start.10 = (bf16[512,2048]{1,0:T(8,128)(2,1)S(1)}, bf16[512,2048]{1,0:T(8,128)(2,1)}, u32[]{:S(2)}) copy-start(bf16[512,2048]{1,0:T(8,128)(2,1)} %all-gather.2.cloned.1.call-done) | copy-start | bytes 6291460
  156.5 4.2 %copy-start.23 = (bf16[512,1024]{1,0:T(8,128)(2,1)S(1)}, bf16[512,1024]{1,0:T(8,128)(2,1)}, u32[]{:S(2)}) copy-start(bf16[512,1024]{1,0:T(8,128)(2,1)} %get-tuple-element.69) | copy-start | bytes 3145732
  160.6 2.7 copy-start.13
  172.7 3.8 %copy-start.5 = (bf16[8192,128]{1,0:T(8,128)(2,1)S(1)}, bf16[8192,128]{1,0:T(8,128)(2,1)}, u32[]{:S(2)}) copy-start(bf16[8192,128]{1,0:T(8,128)(2,1)} %reshape.320) | copy-start | bytes 6291460
  178.1 7.6 %copy-start.15 = (bf16[128,1024]{1,0:T(8,128)(2,1)S(1)}, bf16[128,1024]{1,0:T(8,128)(2,1)}, u32[]{:S(2)}) copy-start(bf16[128,1024]{1,0:T(8,128)(2,1)} %param.10) | copy-start | bytes 786436
  188.1 2.8 copy-start
  190.9 78.1 %copy-start.3 = (f32[1,393344]{1,0:T(1,128)S(1)}, f32[1,393344]{1,0:T(1,128)}, u32[]{:S(2)}) copy-start(f32[1,393344]{1,0:T(1,128)} %param.15) | copy-start | bytes 4720132
  190.9 78.1 %copy-start.4 = (f32[1,393344]{1,0:T(1,128)S(1)}, f32[1,393344]{1,0:T(1,128)}, u32[]{:S(2)}) copy-start(f32[1,393344]{1,0:T(1,128)} %param.17) | copy-start | bytes 4720132
  269.0 3.5 %copy-start.18 = (f32[288]{0:T(512)S(1)}, f32[288]{0:T(512)}, u32[]{:S(2)}) copy-start(f32[288]{0:T(512)} %param.12) | copy-start | bytes 3460
  269.0 3.5 %copy-start.19 = (f32[288]{0:T(512)S(1)}, f32[288]{0:T(512)}, u32[]{:S(2)}) copy-start(f32[288]{0:T(512)} %param.14) | copy-start | bytes 3460
  269.0 3.5 %copy-start.20 = (f32[288]{0:T(512)S(1)}, f32[288]{0:T(512)}, u32[]{:S(2)}) copy-start(f32[288]{0:T(512)} %param.16) | copy-start | bytes 3460
  269.0 4.1 %copy-start.16 = (bf16[128,1024]{1,0:T(8,128)(2,1)S(1)}, bf16[128,1024]{1,0:T(8,128)(2,1)}, u32[]{:S(2)}) copy-start(bf16[128,1024]{1,0:T(8,128)(2,1)} %param.9) | copy-start | bytes 786436
Sparse Core Ops, SparseCore 0:
  10.2 25.2 all-gather.1
  137.6 29.7 reduce-scatter.4
  170.1 32.8 reduce-scatter.2
where the time goes:
time: 286 us; the launch traced here: 281 us
  Pallas kernels  159 us (56%)
  local copies, waits for them, and re-layouts  52.6 us (18%)
  matrix products  41.2 us (14%)
  other arithmetic  14.2 us (5%)
  between operations  14.2 us (5%)
    pallas_call x1, Pallas kernels, reduce_parts(): pl.pallas_call(reduce_kernel, out_shape=(jax.ShapeDtypeStruct((SUM_ROWS,...  78 us
    pallas_call x1, Pallas kernels, gather_parts(): pl.pallas_call(gather_kernel, out_shape=(jax.ShapeDtypeStruct((DP * BLOCK...  77.6 us
    reshape x4, local copies, waits for them, and re-layouts, local_grouped(): part.astype(bf16).reshape(-1, LANES)  13.5 us
    unnamed x59, local copies, waits for them, and re-layouts  12.9 us
    reshape x4, local copies, waits for them, and re-layouts, local_grouped(): full[offsets[k]:offsets[k + 1]].reshape(shape)  12.8 us
    dot_general x1, matrix products, local_grouped(): hidden_pre = jnp.dot(second_low, w_fc, preferred_element_type=f32) + b_fc  6.85 us
    pad x1, local copies, waits for them, and re-layouts, reduce_parts(): flat = jnp.pad(flat, ((0, DP * BLOCK + EDGE - flat.shape[0]), (0, 0)))  6.04 us
  transfers between devices with their start and end apart: 3, of which 0 were waited for; matrix products, arithmetic and copies ran while one was open for 25% of the time, Pallas kernels for 57%

commit v1 on v0

--- a/solution.py
+++ b/solution.py
@@ -404,6 +404,7 @@
 SHARED_ROWS = 8
 PLACE_ROWS = 256
 STEP_ROWS = 448
+CAST_ROWS = 464
 SUM_ROWS = 7 * STEP_ROWS + EDGE
 
 
@@ -578,10 +579,16 @@
 
 
 def reduce_kernel(
-    flat,
+    grad_qkv,
+    grad_dense,
+    grad_fc,
+    grad_bias,
+    grad_proj,
     shared,
     out,
     shared_out,
+    wide,
+    flat,
     x_in,
     up_in,
     down_in,
@@ -602,6 +609,32 @@
     d, s = lax.axis_index("dp"), lax.axis_index("seq")
     z, x = d // 2, lax.rem(d, 2)
     f32 = jnp.float32
+    base = 0
+    for ref in (grad_qkv, grad_dense, grad_fc, grad_bias, grad_proj):
+        count, across_row = ref.shape[0], ref.shape[1] // LANES
+        tile = min(count, 256)
+
+        def spread(k, carry, ref=ref, base=base, across_row=across_row, tile=tile):
+            at = pl.multiple_of(k * tile, tile)
+            to = base + k * tile * across_row
+            for j in range(across_row):
+                part = ref[pl.ds(at, tile), j * LANES : (j + 1) * LANES].astype(f32)
+                if across_row == 1:
+                    wide[pl.ds(to, tile), :] = part
+                else:
+                    wide[pl.ds(to + j, tile, stride=across_row), :] = part
+            return carry
+
+        lax.fori_loop(0, count // tile, spread, 0)
+        base += count * across_row
+    wide[base:, :] = jnp.zeros((wide.shape[0] - base, LANES), f32)
+
+    def narrow(k, carry):
+        at = pl.multiple_of(k * CAST_ROWS, EDGE)
+        flat[pl.ds(at, CAST_ROWS), :] = wide[pl.ds(at, CAST_ROWS), :].astype(flat.dtype)
+        return carry
+
+    lax.fori_loop(0, wide.shape[0] // CAST_ROWS, narrow, 0)
     enter(d, s)
 
     def across(zp, c):
@@ -765,9 +798,8 @@
     shared_out[...] = total
 
 
-def reduce_parts(flat, shared_flat, dp_count, seq_count):
+def reduce_parts(parts, shared_flat, dp_count, seq_count):
     count = shared_flat.shape[0] // (DP * SEQ)
-    flat = jnp.pad(flat, ((0, DP * BLOCK + EDGE - flat.shape[0]), (0, 0)))
     shared = jnp.pad(
         shared_flat.reshape(DP, SEQ, count), ((0, 0), (0, 0), (0, SHARED_ROWS * LANES - count))
     )
@@ -782,9 +814,11 @@
             jax.ShapeDtypeStruct((SUM_ROWS, LANES), jnp.float32),
             jax.ShapeDtypeStruct((SHARED_ROWS, LANES), jnp.float32),
         ),
-        in_specs=[vmem, vmem],
+        in_specs=[vmem] * 6,
         out_specs=(vmem, vmem),
         scratch_shapes=[
+            pltpu.VMEM((DP * BLOCK + EDGE, LANES), jnp.float32),
+            pltpu.VMEM((DP * BLOCK + EDGE, LANES), jnp.bfloat16),
             held,
             held,
             held,
@@ -803,11 +837,11 @@
             dma((DP,)),
         ],
         compiler_params=pltpu.CompilerParams(
-            collective_id=1, has_side_effects=True, vmem_limit_bytes=40 * 2**20
+            collective_id=1, has_side_effects=True, vmem_limit_bytes=52 * 2**20
         ),
         cost_estimate=pl.CostEstimate(flops=0, bytes_accessed=250 * 2**20, transcendentals=0),
         name="reduce_grads",
-    )(flat, shared)
+    )(*parts, shared)
     return out, shared_out.reshape(-1)[:count]
 
 
@@ -1007,13 +1041,14 @@
             jnp.sum(grad_second, 0),
         ]
     )
-    flat = jnp.concatenate(
-        [
-            part.astype(bf16).reshape(-1, LANES)
-            for part in (grad_w_qkv, grad_w_dense, grad_w_fc, grad_b_fc, grad_w_proj)
-        ]
-    )
-    split_sums, shared_grads = reduce_parts(flat, shared_flat, dp_count, seq_count)
+    parts = [
+        grad_w_qkv.astype(bf16),
+        grad_w_dense.astype(bf16),
+        grad_w_fc.astype(bf16),
+        grad_b_fc.reshape(-1, LANES),
+        grad_w_proj.astype(bf16),
+    ]
+    split_sums, shared_grads = reduce_parts(parts, shared_flat, dp_count, seq_count)
     shared_new, shared_m1_new, shared_m2_new = adamw(
         shared_params, shared_m1, shared_m2, shared_grads
     )

time: 286 us -> 281 us (0.983)
  local copies, waits for them, and re-layouts: 52.6 us -> 27.3 us
  waiting for transfers between devices: 0.07 us -> 13 us
  Pallas kernels: 159 us -> 167 us
    reshape x4 -> x0, local copies, waits for them, and re-layouts: 13.5 us -> none  [local_grouped(): part.astype(bf16).reshape(-1, LANES)]
    reduce_scatter x1, waiting for transfers between devices: 0.01 us -> 13 us  [local_grouped(): lax.psum_scatter(gain_one * grad_first + gain_two * grad_second, 'seq', s...]
    pallas_call x1, Pallas kernels: 78 us -> 86.2 us  [reduce_parts(): pl.pallas_call(reduce_kernel, out_shape=(jax.ShapeDtypeStruct((SUM_ROWS,...]
    unnamed x59 -> x51, local copies, waits for them, and re-layouts: 12.9 us -> 6.39 us
    pad x1 -> x0, local copies, waits for them, and re-layouts: 6.04 us -> none  [reduce_parts(): flat = jnp.pad(flat, ((0, DP * BLOCK + EDGE - flat.shape[0]), (0, 0)))]
  transfers between devices with their start and end apart: 3 -> 3, of which waited for: 0 -> 1; matrix products, arithmetic and copies ran while one was open for 25% -> 15% of each run, Pallas kernels for 57% -> 61%
where the time goes in v1:
time: 281 us; the launch traced here: 276 us
  Pallas kernels  167 us (59%)
  matrix products  40.2 us (14%)
  local copies, waits for them, and re-layouts  27.3 us (10%)
  other arithmetic  14.2 us (5%)
  between operations  14.2 us (5%)
  waiting for transfers between devices  13 us (5%)
    pallas_call x1, Pallas kernels, reduce_parts(): pl.pallas_call(reduce_kernel, out_shape=(jax.ShapeDtypeStruct((SUM_ROWS,...  86.2 us
    pallas_call x1, Pallas kernels, gather_parts(): pl.pallas_call(gather_kernel, out_shape=(jax.ShapeDtypeStruct((DP * BLOCK...  77.6 us
    reduce_scatter x1, waiting for transfers between devices, local_grouped(): lax.psum_scatter(gain_one * grad_first + gain_two * grad_second, 'seq', s...  13 us
    reshape x4, local copies, waits for them, and re-layouts, local_grouped(): full[offsets[k]:offsets[k + 1]].reshape(shape)  12 us
    dot_general x1, matrix products, local_grouped(): hidden_pre = jnp.dot(second_low, w_fc, preferred_element_type=f32) + b_fc  6.84 us
    unnamed x51, local copies, waits for them, and re-layouts  6.39 us
  transfers between devices with their start and end apart: 3, of which 1 were waited for; matrix products, arithmetic and copies ran while one was open for 15% of the time, Pallas kernels for 61%

profile of v1, /device:TPU:0, one launch (start us, length us, event | category | flops | bytes accessed | tf_op | source)
XLA Modules:
  0.0 276.3 jit_solution(2488270989517149569)
XLA Ops:
  7.2 2.0 pad_maximum_fusion
  9.3 0.7 pad_bitcast_fusion.1.shared
  10.0 77.6 %gather_params.1 = (bf16[24592,128]{1,0:T(8,128)(2,1)S(1)}, f32[8,4,8,128]{3,2,1,0:T(8,128)S(1)}) custom-call(f32[3073,1,128]{2,1,0:T(1,128)S(1)} %bitcast.88, f32[8,128]{1,0:T(8,128)S(1)} %pad_bitcast_fusion.1.shared), custom_call_target="tpu_custom_call" | custom-call | bytes 209715200 | tf_op jit(solution)/shard_map/gather_params/pallas_call | solution.py:549
  87.6 0.1 slice.116
  87.7 2.5 copy-done.1
  90.2 0.8 slice.131
  91.1 0.1 reshape.295
  91.2 2.3 reshape.296
  93.5 0.1 compare_reduce_fusion
  93.5 0.1 add_select_fusion
  93.6 0.3 reduce-window.9
  93.9 0.1 slice.122
  94.0 1.3 reshape.300
  95.3 4.5 %fusion.44 = (bf16[8192,128]{1,0:T(8,128)(2,1)}, bf16[8192,128]{1,0:T(8,128)(2,1)}) fusion(bf16[24592,128]{1,0:T(8,128)(2,1)} %copy-done.1), kind=kLoop, calls=%fused_computation.126 | loop fusion | bytes 8388608 | tf_op jit(solution)/shard_map/slice | solution.py:961
  99.8 4.2 %reshape.301 = bf16[1024,1024]{1,0:T(8,128)(2,1)} reshape(bf16[8192,128]{1,0:T(8,128)(2,1)} %get-tuple-element.39) | data formatting | bytes 4194304 | tf_op jit(solution)/shard_map/reshape | solution.py:961
  104.1 4.2 %reshape.302 = bf16[1024,1024]{1,0:T(8,128)(2,1)} reshape(bf16[8192,128]{1,0:T(8,128)(2,1)} %get-tuple-element.38) | data formatting | bytes 4194304 | tf_op jit(solution)/shard_map/reshape | solution.py:961
  108.3 0.1 dynamic_slice.7
  108.4 0.1 slice_reduce_fusion
  108.5 0.1 fusion.33
  108.6 0.7 bitcast_convert_fusion
  109.2 0.1 broadcast_multiply_fusion
  109.4 0.2 fusion.21
  109.6 1.6 convert_reduce_fusion
  111.2 1.6 fusion.4
  112.9 3.4 %add_convert_fusion.2 = bf16[512,768]{1,0:T(8,128)(2,1)} fusion(bf16[1024,768]{1,0:T(8,128)(2,1)} %reshape.296, f32[768]{0:T(1024)S(1)} %dynamic_slice.7, f32[1024]{0:T(1024)S(1)} %get-tuple-element.60, f32[1024]{0:T(1024)S(1)} %get-tuple-element.61, f32[512]{0:T(512)S(1)} %add_rsqrt_fusion, f32[512]{0:T(512)S(1)} %broadcast_multiply_fusion.1, ...), kind=kOutput, calls=%fused_computation.46 | convolution fusion | flops 809238528 | bytes 3424256 | tf_op jit(solution)/shard_map/dot_general | solution.py:975
  116.3 1.4 copy.34
  117.7 0.1 copy.53
  117.8 0.2 fusion.37
  118.0 0.9 fusion.1
  119.0 0.9 exponential_reduce_fusion
  119.9 0.7 copy-done.6
  120.6 0.5 convolution_convert_fusion.6
  121.0 1.3 multiply_reduce_fusion.3
  122.4 1.6 multiply_convert_fusion
  124.0 0.7 fusion.31
  124.8 0.5 fusion.29
  125.2 1.3 fusion.20
  126.7 0.2 convert_reduce_fusion.1
  126.9 0.1 copy.41
  126.9 1.1 copy-done.10
  128.0 1.0 fusion.48
  129.1 0.6 copy-done.9
  129.6 6.8 %fusion.7 = (bf16[512,1024]{1,0:T(8,128)(2,1)}, f32[512,1024]{1,0:T(8,128)S(1)}) fusion(f32[1024]{0:T(1024)S(1)} %bitcast_convert_fusion, bf16[1024,1024]{1,0:T(8,128)(2,1)S(1)} %copy-done.9, f32[1024]{0:T(1024)S(1)} %get-tuple-element.58, f32[1024]{0:T(1024)S(1)} %get-tuple-element.59, f32[512]{0:T(512)S(1)} %add_rsqrt_fusion, ...), kind=kOutput, calls=%fused_computation.15 | convolution fusion | flops 1111490560 | bytes 6307840 | tf_op jit(solution)/shard_map/dot_general | solution.py:986
  136.5 2.1 fusion.46
  138.6 3.8 %multiply_reduce_fusion = (f32[1024]{0:T(1024)S(1)}, f32[1024]{0:T(1024)S(1)}, f32[1024]{0:T(1024)S(1)}, f32[1024]{0:T(1024)S(1)}, f32[512,1024]{1,0:T(8,128)}, /*index=5*/f32[512,1024]{1,0:T(8,128)}) fusion(f32[512]{0:T(512)S(1)} %add_rsqrt_fusion, f32[512]{0:T(512)S(1)} %broadcast_multiply_fusion.1, bf16[512,2048]{1,0:T(8,128)(2,1)S(1)} %copy-done.6, ...), kind=kOutput, calls=%fused_computation.21 | convolution fusion | flops 1080029184 | bytes 10514432 | tf_op jit(solution)/shard_map/dot_general | solution.py:1001
  142.5 3.2 %fusion.47 = f32[512,1024]{1,0:T(8,128)S(1)} fusion(bf16[512,1024]{1,0:T(8,128)(2,1)} %get-tuple-element.69, bf16[1024,1024]{1,0:T(8,128)(2,1)} %reshape.302), kind=kOutput, calls=%fused_computation.129 | convolution fusion | flops 1073741824 | bytes 5242880 | tf_op jit(solution)/shard_map/dot_general | solution.py:988
  145.7 1.8 convolution_add_fusion
  147.5 0.1 dynamic-slice.3
  147.6 0.1 reduce_sum.127
  147.7 0.5 dynamic_update_slice.3
  148.2 1.8 convolution_convert_fusion.3.grad_dense
  150.1 3.8 %convolution_convert_fusion.2.grad_qkv = bf16[1024,768]{1,0:T(8,128)(2,1)} fusion(bf16[512,768]{0,1:T(8,128)(2,1)S(1)} %bitcast.100, f32[1024]{0:T(1024)S(1)} %get-tuple-element.60, f32[1024]{0:T(1024)S(1)} %get-tuple-element.61, f32[512]{0:T(512)S(1)} %add_rsqrt_fusion, f32[512]{0:T(512)S(1)} %broadcast_multiply_fusion.1, ...), kind=kOutput, calls=%fused_computation.43 | convolution fusion | flops 809238528 | bytes 3420160 | tf_op jit(solution)/shard_map/dot_general | solution.py:1021
  153.9 2.7 convolution_convert_fusion.grad_proj
  156.6 2.8 %convolution_convert_fusion.1.grad_fc = bf16[1024,1024]{1,0:T(8,128)(2,1)} fusion(bf16[512,1024]{1,0:T(8,128)(2,1)S(1)} %copy-done.20, f32[1024]{0:T(1024)S(1)} %get-tuple-element.58, f32[1024]{0:T(1024)S(1)} %get-tuple-element.59, f32[512]{0:T(512)S(1)} %add_rsqrt_fusion, f32[512]{0:T(512)S(1)} %broadcast_multiply_fusion.1, bf16[512,2048]{1,0:T(8,128)(2,1)S(1)} %copy-done.7), kind=kOutput, calls=%fused_computation.42 | convolution fusion | flops 1077936128 | bytes 4206592 | tf_op jit(solution)/shard_map/dot_general | solution.py:1000
  159.4 13.0 %reduce-scatter.5.cloned.1.call-done = f32[128,1024]{1,0:T(8,128)} async-done(((f32[512,1024]{1,0:T(8,128)}), f32[128,1024]{1,0:T(8,128)}) %reduce-scatter.5.cloned.1.call-update) | async-done | bytes 524304 | tf_op jit(solution)/shard_map/reduce_scatter | solution.py:1024
  172.4 1.3 fusion.42
  173.7 2.2 convert_reduce_fusion.2
  176.0 0.1 reshape.306
  176.1 0.1 reshape.317
  176.2 86.2 %reduce_grads.1 = (f32[3152,128]{1,0:T(8,128)}, f32[8,128]{1,0:T(8,128)S(1)}) custom-call(bf16[1024,768]{1,0:T(8,128)(2,1)} %convolution_convert_fusion.2.grad_qkv, bf16[256,1024]{1,0:T(8,128)(2,1)S(1)} %convolution_convert_fusion.3.grad_dense, bf16[1024,1024]{1,0:T(8,128)(2,1)} %convolution_convert_fusion.1.grad_fc, f32[8,128]{1,0:T(8,128)S(1)} %bitcast.93, ...), custom_call_target="tpu_custom_call" | custom-call | bytes 262144000 | tf_op jit(solution)/shard_map/reduce_grads/pallas_call | solution.py:811
  262.4 1.4 copy-done.2
  263.8 3.4 %adamw_rows.1 = (f32[3073,1,128]{2,1,0:T(1,128)}, f32[3073,1,128]{2,1,0:T(1,128)}, f32[3073,1,128]{2,1,0:T(1,128)}, f32[3073,1,128]{2,1,0:T(1,128)}) custom-call(s32[1]{0:T(128)} %bitcast.25.where, f32[3152,128]{1,0:T(8,128)S(1)} %copy-done.2, f32[3073,1,128]{2,1,0:T(1,128)S(1)} %bitcast.89, f32[3073,1,128]{2,1,0:T(1,128)S(1)} %bitcast.90, ...), custom_call_target="tpu_custom_call" | custom-call | tf_op jit(solution)/shard_map/adamw_rows/pallas_call | solution.py:883
  267.3 0.6 multiply_subtract_fusion
  267.9 1.8 add_convert_fusion.3
  (77 shorter events, 0.7 us)
Async XLA Ops:
  7.2 2.8 %copy-start = (f32[1,393344]{1,0:T(1,128)S(1)}, f32[1,393344]{1,0:T(1,128)}, u32[]{:S(2)}) copy-start(f32[1,393344]{1,0:T(1,128)} %param.13) | copy-start | bytes 4720132
  7.2 102.4 %all-gather.2.cloned.1.call-start = ((), (), s32[]{:S(2)}) async-start(), calls=%async_computation.2 | async-start | bytes 2621440 | tf_op jit(solution)/shard_map/all_gather | solution.py:952
  9.2 163.1 %reduce-scatter.5.cloned.1.call-start = ((), (), s32[]{:S(2)}) async-start(), calls=%async_computation.4 | async-start | bytes 2621440 | tf_op jit(solution)/shard_map/reduce_scatter | solution.py:1024
  87.5 2.7 copy-start.1
  90.2 3.2 %copy-start.15 = (s32[1,512]{1,0:T(1,128)S(1)}, s32[1,512]{1,0:T(1,128)}, u32[]{:S(2)}) copy-start(s32[1,512]{1,0:T(1,128)} %param.11) | copy-start | bytes 6148
  91.2 4.1 %copy-start.13 = (f32[9216]{0:T(1024)}, f32[9216]{0:T(1024)S(1)}, u32[]{:S(2)}) copy-start(f32[9216]{0:T(1024)S(1)} %reshape.295) | copy-start | bytes 110596
  104.0 4.2 %slice-start = ((f32[9216]{0:T(1024)}), f32[3072]{0:T(1024)S(1)}, s32[]{:S(2)}) async-start(f32[9216]{0:T(1024)} %copy-done.13), calls=%async_computation.5 | async-start | bytes 24576 | tf_op jit(solution)/shard_map/slice | solution.py:42
  104.0 5.2 %copy-start.14 = (f32[9216]{0:T(1024)S(1)}, f32[9216]{0:T(1024)}, u32[]{:S(2)}) copy-start(f32[9216]{0:T(1024)} %copy-done.13) | copy-start | bytes 110596
  109.6 3.3 %copy-start.5 = (bf16[512,2048]{1,0:T(8,128)(2,1)S(1)}, bf16[512,2048]{1,0:T(8,128)(2,1)}, u32[]{:S(2)}) copy-start(bf16[512,2048]{1,0:T(8,128)(2,1)} %all-gather.2.cloned.1.call-done) | copy-start | bytes 6291460
  119.0 1.6 copy-start.6
  126.6 1.4 copy-start.10
  128.0 1.6 copy-start.9
  129.6 6.8 %copy-start.8 = (bf16[1024,1024]{1,0:T(8,128)(2,1)S(1)}, bf16[1024,1024]{1,0:T(8,128)(2,1)}, u32[]{:S(2)}) copy-start(bf16[1024,1024]{1,0:T(8,128)(2,1)} %reshape.302) | copy-start | bytes 6291460
  138.6 3.8 %copy-start.19 = (bf16[512,1024]{1,0:T(8,128)(2,1)}, bf16[512,1024]{1,0:T(8,128)(2,1)S(1)}, u32[]{:S(2)}) copy-start(bf16[512,1024]{1,0:T(8,128)(2,1)S(1)} %get-tuple-element.76) | copy-start | bytes 3145732
  142.5 125.4 %reduce-scatter.3.cloned.1.call-start = ((), (), s32[]{:S(2)}) async-start(), calls=%async_computation.3 | async-start | bytes 2621440 | tf_op jit(solution)/shard_map/reduce_scatter | solution.py:991
  150.0 3.8 %copy-start.7 = (bf16[512,2048]{1,0:T(8,128)(2,1)S(1)}, bf16[512,2048]{1,0:T(8,128)(2,1)}, u32[]{:S(2)}) copy-start(bf16[512,2048]{1,0:T(8,128)(2,1)} %all-gather.2.cloned.1.call-done) | copy-start | bytes 6291460
  150.0 3.8 %copy-start.21 = (bf16[512,1024]{1,0:T(8,128)(2,1)S(1)}, bf16[512,1024]{1,0:T(8,128)(2,1)}, u32[]{:S(2)}) copy-start(bf16[512,1024]{1,0:T(8,128)(2,1)} %get-tuple-element.69) | copy-start | bytes 3145732
  153.9 2.7 copy-start.20
  156.6 17.2 %copy-start.11 = (bf16[128,1024]{1,0:T(8,128)(2,1)S(1)}, bf16[128,1024]{1,0:T(8,128)(2,1)}, u32[]{:S(2)}) copy-start(bf16[128,1024]{1,0:T(8,128)(2,1)} %param.10) | copy-start | bytes 786436
  176.2 86.2 %copy-start.3 = (f32[1,393344]{1,0:T(1,128)S(1)}, f32[1,393344]{1,0:T(1,128)}, u32[]{:S(2)}) copy-start(f32[1,393344]{1,0:T(1,128)} %param.15) | copy-start | bytes 4720132
  176.2 86.2 %copy-start.4 = (f32[1,393344]{1,0:T(1,128)S(1)}, f32[1,393344]{1,0:T(1,128)}, u32[]{:S(2)}) copy-start(f32[1,393344]{1,0:T(1,128)} %param.17) | copy-start | bytes 4720132
  262.4 1.4 copy-start.2
  263.8 3.4 %copy-start.16 = (f32[288]{0:T(512)S(1)}, f32[288]{0:T(512)}, u32[]{:S(2)}) copy-start(f32[288]{0:T(512)} %param.12) | copy-start | bytes 3460
  263.8 3.4 %copy-start.17 = (f32[288]{0:T(512)S(1)}, f32[288]{0:T(512)}, u32[]{:S(2)}) copy-start(f32[288]{0:T(512)} %param.14) | copy-start | bytes 3460
  263.8 3.4 %copy-start.18 = (f32[288]{0:T(512)S(1)}, f32[288]{0:T(512)}, u32[]{:S(2)}) copy-start(f32[288]{0:T(512)} %param.16) | copy-start | bytes 3460
  263.8 4.1 %copy-start.12 = (bf16[128,1024]{1,0:T(8,128)(2,1)S(1)}, bf16[128,1024]{1,0:T(8,128)(2,1)}, u32[]{:S(2)}) copy-start(bf16[128,1024]{1,0:T(8,128)(2,1)} %param.9) | copy-start | bytes 786436
Sparse Core Ops, SparseCore 0:
  10.2 25.2 all-gather.1
  142.6 29.7 reduce-scatter.4
  175.1 31.4 reduce-scatter.2
